TPU v7x, 32 devices: a whole 2x2x4 slice. The times are simulated.
32 devices in a mesh: rep: 4 (over y, core), shard: 4 (over z), tp: 2 (over x).
Axes of the slice: x: 2, y: 2, z: 4, core: 2. Of those that a mesh axis runs over, the one named last changes fastest.
Arguments:
- hidden_in: bfloat16 [8192, 8192], P(('rep', 'shard', 'tp')), may hold values from -6 to 6
- lengths: int32 [16], P(('rep', 'shard')), may hold values from 128 to 512, as said below
- kv_grad_out: bfloat16 [8192, 2, 1024], P(('rep', 'shard'), None, 'tp'), may hold values from -384 to 384
- master: float32 [8192, 2, 1024], P('shard', None, 'tp'), may hold values from -0.0625 to 0.0625
- moment_one: float32 [8192, 2, 1024], P('shard', None, 'tp'), may hold values from -3 to 3
- moment_two: float32 [8192, 2, 1024], P('shard', None, 'tp'), may hold values from 0.05 to 2
Outputs:
- new_master: float32 [8192, 2, 1024], P('shard', None, 'tp')
- new_moment_one: float32 [8192, 2, 1024], P('shard', None, 'tp')
- new_moment_two: float32 [8192, 2, 1024], P('shard', None, 'tp')
- fresh_kv: bfloat16 [8192, 2, 1024], P(('rep', 'shard'), None, 'tp')
Inputs may be any that keep to these rules, and one draw needn't show every extreme that they name: In block b only its first lengths[b] tokens are valid.
All inputs are finite; a program needn't handle non-finite values.
Results may differ from a plain program's by a relative error of at most 0.014.
Values may be sent and summed in bfloat16 or wider, within the bound.
No kernel may reach another device: no remote copies, remote signals or barrier semaphores. Data moves between devices by JAX's collectives and lax.ppermute only.
A program may use at most 192 MiB of HBM per device.

v0:
```python
import jax
import jax.numpy as jnp
from jax import lax
from jax.sharding import PartitionSpec as P

beta_one = 0.9
beta_two = 0.95
step_count = 20
rate = 0.002
decay = 0.1
epsilon = 1e-08


def adamw(master, moment_one, moment_two, grad):
    first = beta_one * moment_one + (1.0 - beta_one) * grad
    second = beta_two * moment_two + (1.0 - beta_two) * grad * grad
    first_hat = first / (1.0 - beta_one**step_count)
    second_hat = second / (1.0 - beta_two**step_count)
    updated = master - rate * (first_hat / (jnp.sqrt(second_hat) + epsilon) + decay * master)
    return (updated, first, second)


def local(hidden_in, lengths, kv_grad_out, master, moment_one, moment_two):
    gathered = lax.all_gather(hidden_in, "tp", axis=0, tiled=True)
    tokens_here = gathered.shape[0]
    features = kv_grad_out.shape[2]
    validity = (jnp.arange(tokens_here, dtype=jnp.int32) < lengths[0]).astype(kv_grad_out.dtype)
    cotan = (kv_grad_out * validity[:, None, None]).reshape(tokens_here, 2 * features)
    local_count = jnp.sum(lengths.astype(jnp.float32))
    count = lax.psum(local_count, ("rep", "shard"))
    contract = (((0,), (0,)), ((), ()))
    columns = gathered
    shard_grad = lax.psum_scatter(
        lax.dot_general(columns, cotan, contract, preferred_element_type=jnp.float32).astype(
            jnp.bfloat16
        ),
        "shard",
        scatter_dimension=0,
        tiled=True,
    )
    summed = lax.psum(shard_grad, "rep").astype(jnp.float32)
    grad = summed.reshape(master.shape) / count
    new_master, new_first, new_second = adamw(master, moment_one, moment_two, grad)
    weights = new_master.astype(jnp.bfloat16)
    piece = lax.all_gather(weights, "shard", axis=0, tiled=True)
    columns = gathered
    flat_piece = piece.reshape(piece.shape[0], 2 * features)
    fresh = jnp.dot(columns, flat_piece, preferred_element_type=jnp.float32)
    fresh_kv = fresh.astype(jnp.bfloat16).reshape(tokens_here, 2, features)
    return (new_master, new_first, new_second, fresh_kv)


def solution(mesh):
    in_specs = (
        P(("rep", "shard", "tp"), None),
        P(("rep", "shard")),
        P(("rep", "shard"), None, "tp"),
        P("shard", None, "tp"),
        P("shard", None, "tp"),
        P("shard", None, "tp"),
    )
    out_specs = (
        P("shard", None, "tp"),
        P("shard", None, "tp"),
        P("shard", None, "tp"),
        P(("rep", "shard"), None, "tp"),
    )
    return jax.shard_map(local, mesh=mesh, in_specs=in_specs, out_specs=out_specs, check_vma=False)
```

profile of v0, /device:TPU:0, one launch (start us, length us, event | category | flops | bytes accessed | tf_op | source)
XLA Modules:
  0.0 888.6 jit_solution(11009722676613736026)
XLA Ops:
  7.2 0.0 all-gather.3.cloned.1.call-start
  7.2 0.7 all-gather.3.cloned.1.call-update
  7.9 0.0 reduce-scatter.2.cloned.1.call-start
  8.6 2.9 broadcast_multiply_fusion
  11.5 0.2 copy.39
  11.7 104.6 %all-gather.3.cloned.1.call-done = bf16[512,8192]{1,0:T(8,128)(2,1)} async-done(((bf16[256,8192]{1,0:T(8,128)(2,1)}), bf16[512,8192]{1,0:T(8,128)(2,1)}) %all-gather.3.cloned.1.call-update) | async-done | bytes 8388624 | tf_op jit(solution)/shard_map/all_gather | solution.py:24
  116.3 15.8 %convert_bitcast_fusion = bf16[8192,1024]{0,1:T(8,128)(2,1)} fusion(bf16[512,1024]{1,0:T(8,128)(2,1)S(1)} %bitcast.23, bf16[512,8192]{1,0:T(8,128)(2,1)} %all-gather.3.cloned.1.call-done), kind=kOutput, calls=%fused_computation | convolution fusion | flops 8598323200 | bytes 26214400 | tf_op jit(solution)/shard_map/dot_general | solution.py:34
  132.0 0.0 reduce-scatter.2.cloned.1.call-update
  132.1 0.0 all-reduce.2.cloned.1.call-start
  132.1 280.4 %reduce-scatter.2.cloned.1.call-done = bf16[2048,1024]{0,1:T(8,128)(2,1)} async-done(((bf16[8192,1024]{0,1:T(8,128)(2,1)}), bf16[2048,1024]{0,1:T(8,128)(2,1)}) %reduce-scatter.2.cloned.1.call-update) | async-done | bytes 4194320 | tf_op jit(solution)/shard_map/reduce_scatter | solution.py:33
  412.5 0.0 all-reduce.2.cloned.1.call-update
  412.6 0.0 all-gather.5.cloned.1.call-start
  412.6 35.1 %psum.15 = f32[]{:T(128)} all-reduce(f32[]{:T(128)} %bitcast.2), channel_id=1, replica_groups=mesh['rep'=4,'shard'=4,'tp'=2] {'rep','shard'}, use_global_device_ids=true, to_apply=%region_2.0 | all-reduce | flops 1 | bytes 8 | tf_op jit(solution)/shard_map/psum | solution.py:30
  447.7 53.8 %all-reduce.2.cloned.1.call-done = bf16[2048,1024]{0,1:T(8,128)(2,1)} async-done(((bf16[2048,1024]{0,1:T(8,128)(2,1)}), bf16[2048,1024]{0,1:T(8,128)(2,1)}) %all-reduce.2.cloned.1.call-update) | async-done | bytes 4194320 | tf_op jit(solution)/shard_map/psum | solution.py:41
  501.5 7.4 convert_divide_fusion
  509.0 8.7 copy.28
  517.7 24.7 %fusion.3 = (bf16[2048,2,512]{2,0,1:T(8,128)(2,1)S(1)}, f32[2048,2,512]{2,0,1:T(8,128)}, f32[2048,2,512]{2,0,1:T(8,128)}, f32[2048,2,512]{2,0,1:T(8,128)}) fusion(f32[2048,2,512]{2,1,0:T(2,128)} %param.9, f32[2048,2,512]{2,0,1:T(8,128)} %copy.28, f32[2048,2,512]{2,1,0:T(2,128)} %param.10, f32[2048,2,512]{2,1,0:T(2,128)} %param.11), kind=kLoop, calls=%fused_computation.12 | loop fusion | flops 33554432 | bytes 62914560 | tf_op jit(solution)/shard_map/convert_element_type | solution.py:44
  542.4 19.0 %copy.34 = bf16[2048,2,512]{2,1,0:T(2,128)(2,1)} copy(bf16[2048,2,512]{2,0,1:T(8,128)(2,1)S(1)} %get-tuple-element.20) | data formatting | bytes 8388608 | tf_op jit(solution)/shard_map/convert_element_type | solution.py:44
  561.4 0.0 all-gather.5.cloned.1.call-update
  561.4 0.0 slice-start
  561.4 15.5 %copy.35 = f32[2048,2,512]{2,1,0:T(2,128)} copy(f32[2048,2,512]{2,0,1:T(8,128)} %get-tuple-element.21) | data formatting | bytes 16777216
  576.9 0.0 slice-start.1
  576.9 15.6 %copy.36 = f32[2048,2,512]{2,1,0:T(2,128)} copy(f32[2048,2,512]{2,0,1:T(8,128)} %get-tuple-element.22) | data formatting | bytes 16777216
  592.6 0.0 slice-done
  592.6 0.0 slice-done.1
  592.6 16.7 %copy.37 = f32[2048,2,512]{2,1,0:T(2,128)} copy(f32[2048,2,512]{2,0,1:T(8,128)S(1)} %bitcast.18) | data formatting | bytes 16777216
  609.3 239.2 %all-gather.5.cloned.1.call-done = bf16[8192,2,512]{2,1,0:T(2,128)(2,1)} async-done(((bf16[2048,2,512]{2,1,0:T(2,128)(2,1)}), bf16[8192,2,512]{2,1,0:T(2,128)(2,1)}) %all-gather.5.cloned.1.call-update) | async-done | bytes 16777232 | tf_op jit(solution)/shard_map/all_gather | solution.py:45
  848.5 16.6 %copy.40 = bf16[1024,8,2,512]{3,1,2,0:T(8,128)(2,1)} copy(bf16[1024,8,2,512]{3,2,1,0:T(2,128)(2,1)} %bitcast.20) | data formatting | bytes 33554432
  865.0 14.9 %convolution_convert_fusion = bf16[1024,512]{1,0:T(8,128)(2,1)S(1)} fusion(bf16[8192,1024]{1,0:T(8,128)(2,1)} %bitcast.21, bf16[512,8192]{1,0:T(8,128)(2,1)} %all-gather.3.cloned.1.call-done), kind=kOutput, calls=%fused_computation.8 | convolution fusion | flops 8590458880 | bytes 26214400 | tf_op jit(solution)/shard_map/dot_general | solution.py:48
  879.9 2.1 copy.38
  (2 shorter events, 0.0 us)
Async XLA Ops:
  7.2 109.1 %all-gather.3.cloned.1.call-start = ((), (), s32[]{:S(2)}) async-start(), calls=%async_computation.1 | async-start | bytes 12582912 | tf_op jit(solution)/shard_map/all_gather | solution.py:24
  7.9 404.6 %reduce-scatter.2.cloned.1.call-start = ((), (), s32[]{:S(2)}) async-start(), calls=%async_computation.2 | async-start | bytes 20971520 | tf_op jit(solution)/shard_map/reduce_scatter | solution.py:33
  132.1 369.5 %all-reduce.2.cloned.1.call-start = ((), (), s32[]{:S(2)}) async-start(), calls=%async_computation.3 | async-start | bytes 8388608 | tf_op jit(solution)/shard_map/psum | solution.py:41
  412.6 435.9 %all-gather.5.cloned.1.call-start = ((), (), s32[]{:S(2)}) async-start(), calls=%async_computation.4 | async-start | bytes 20971520 | tf_op jit(solution)/shard_map/all_gather | solution.py:45
  561.4 31.2 %slice-start = ((s8[8388608]{0:T(1024)(128)(4,1)}), s8[4194304]{0:T(1024)(128)(4,1)S(1)}, s32[]{:S(2)}) async-start(s8[8388608]{0:T(1024)(128)(4,1)} %bitcast.17), calls=%async_computation.5 | async-start | bytes 8388608
  576.9 15.6 %slice-start.1 = ((s8[8388608]{0:T(1024)(128)(4,1)}), s8[4194304]{0:T(1024)(128)(4,1)S(1)}, s32[]{:S(2)}) async-start(s8[8388608]{0:T(1024)(128)(4,1)} %bitcast.17), calls=%async_computation.6 | async-start | bytes 8388608
Sparse Core Ops, SparseCore 0:
  9.5 106.6 all-gather.2
  132.2 280.2 reduce-scatter.1
  415.0 86.4 all-reduce.1
  561.5 286.9 all-gather.4
where the time goes:
time: 889 us
  waiting for transfers between devices  679 us (76%)
  local copies, waits for them, and re-layouts  94.4 us (11%)
  blocking collectives  35.1 us (4%)
  other arithmetic  35 us (4%)
  matrix products  30.7 us (3%)
  between operations  14.5 us (2%)
    reduce_scatter x1, waiting for transfers between devices, local(): lax.psum_scatter(lax.dot_general(columns, cotan, contract, preferred_elem...  280 us
    all_gather x1, waiting for transfers between devices, local(): piece = lax.all_gather(weights, 'shard', axis=0, tiled=True)  239 us
    all_gather x1, waiting for transfers between devices, local(): gathered = lax.all_gather(hidden_in, 'tp', axis=0, tiled=True)  105 us
    unnamed x10, local copies, waits for them, and re-layouts  66.8 us
    psum x1, waiting for transfers between devices, local(): summed = lax.psum(shard_grad, 'rep').astype(jnp.float32)  53.8 us
    psum x1, blocking collectives, local(): count = lax.psum(local_count, ('rep', 'shard'))  35.1 us
    convert_element_type x1, other arithmetic, local(): weights = new_master.astype(jnp.bfloat16)  24.7 us
    convert_element_type x1, local copies, waits for them, and re-layouts, local(): weights = new_master.astype(jnp.bfloat16)  19 us
  transfers between devices with their start and end apart: 4, of which 4 were waited for; matrix products, arithmetic and copies ran while one was open for 6% of the time, Pallas kernels for 0%

commit v1 on v0

v1 whole, which is shorter than its diff:
```python
import functools

import jax
import jax.numpy as jnp
from jax import lax
from jax.experimental import pallas as pl
from jax.experimental.pallas import tpu as pltpu
from jax.sharding import PartitionSpec as P

beta_one = 0.9
beta_two = 0.95
step_count = 20
rate = 0.002
decay = 0.1
epsilon = 1e-08

LANES = 128
GROUPS = 4
VMEM_BYTES = 56 * 1024 * 1024

SMEM = pl.BlockSpec(memory_space=pltpu.SMEM)


def adamw(master, moment_one, moment_two, grad):
    first = beta_one * moment_one + (1.0 - beta_one) * grad
    second = beta_two * moment_two + (1.0 - beta_two) * grad * grad
    first_hat = first / (1.0 - beta_one**step_count)
    second_hat = second / (1.0 - beta_two**step_count)
    updated = master - rate * (first_hat / (jnp.sqrt(second_hat) + epsilon) + decay * master)
    return (updated, first, second)


def lane_rows(array):
    rows, two, features = array.shape
    split = array.reshape(rows, two, features // LANES, LANES)
    return split.transpose(0, 2, 1, 3).reshape(rows * two * features // LANES, LANES)


def from_lane_rows(array, rows, features):
    split = array.reshape(rows, features // LANES, 2, LANES)
    return split.transpose(0, 2, 1, 3).reshape(rows, 2, features)


def slots(features):
    return [half * features + tile * LANES for tile in range(features // LANES) for half in range(2)]


def call(kernel, out_shape, flops, moved, **kwargs):
    return pl.pallas_call(
        kernel,
        out_shape=out_shape,
        cost_estimate=pl.CostEstimate(flops=flops, bytes_accessed=moved, transcendentals=0),
        compiler_params=pltpu.CompilerParams(vmem_limit_bytes=VMEM_BYTES),
        **kwargs,
    )


def full(shape):
    return pl.BlockSpec(shape, lambda *_: (0,) * len(shape))


def f32(ref):
    return ref[...].astype(jnp.float32)


def pack(hidden, rep, groups, replicas, rows):
    tokens = hidden.shape[0]
    specs, shapes, orders = [], [], []
    for start, part, order in groups:
        for k in range(replicas):
            for s in range(len(order)):

                def index(i, place, at=1 + len(orders) + s, k=k, start=start, part=part):
                    return (0, (place[at] * replicas + (place[0] ^ k)) * (rows // part) + start // part)

                specs.append(pl.BlockSpec((tokens, part), index))
            shapes.append((tokens, len(order) * part))
        orders += order

    def kernel(place, *refs):
        sources, outs = iter(refs[: len(specs)]), iter(refs[len(specs) :])
        for start, part, order in groups:
            for k in range(replicas):
                out = next(outs)
                for s in range(len(order)):
                    out[:, s * part : (s + 1) * part] = next(sources)[...]

    outs = call(
        kernel,
        [jax.ShapeDtypeStruct(shape, hidden.dtype) for shape in shapes],
        0,
        4 * sum(shape[0] * shape[1] for shape in shapes),
        grid_spec=pltpu.PrefetchScalarGridSpec(
            num_scalar_prefetch=1,
            grid=(1,),
            in_specs=specs,
            out_specs=[full(shape) for shape in shapes],
        ),
    )(jnp.stack([rep, *orders]), *[hidden] * len(specs))
    return [outs[i : i + replicas] for i in range(0, len(outs), replicas)]


def mask(cotan, place, pairs):
    block, _, features = cotan.shape
    width, tokens = 2 * features, block // pairs
    per = width // LANES

    def kernel(place, source, out, count, scratch):
        scratch[...] = source[...].astype(jnp.float32)
        count[...] = jnp.full(count.shape, place[0]).astype(jnp.float32)
        for o in range(pairs):
            start = (place[1] ^ o) * tokens
            row = lax.broadcasted_iota(jnp.int32, (tokens, LANES), 0) + start
            for slot, column in enumerate(slots(features)):
                rows = scratch[pl.ds(start * per + slot, tokens, stride=per), :]
                out[o * tokens : (o + 1) * tokens, column : column + LANES] = jnp.where(
                    row < place[0], rows, 0.0
                ).astype(out.dtype)

    return call(
        kernel,
        [jax.ShapeDtypeStruct((block, width), cotan.dtype), jax.ShapeDtypeStruct((8, LANES), jnp.float32)],
        0,
        4 * block * width,
        grid=(1,),
        in_specs=[SMEM, full((block * per, LANES))],
        out_specs=[full((block, width)), full((8, LANES))],
        scratch_shapes=[pltpu.VMEM((block * per, LANES), jnp.float32)],
    )(place, lane_rows(cotan))


def fresh_weights(place, count, shares, params):
    part, width = shares[0][1].block_shape
    per = width // LANES

    def kernel(place, count, *refs):
        sources = refs[: len(shares)]
        master, first, second, weights, grad, scratch = refs[len(shares) :]
        grad[...] = sum(f32(source) for source in sources).astype(grad.dtype)
        scale = 1.0 / count[0:1, 0:1]
        starts = slots(width // 2)
        for slot, start in enumerate(starts):
            scratch[pl.ds(slot, part, stride=per), :] = grad[:, start : start + LANES].astype(jnp.float32)
        updated, _, _ = adamw(master[...], first[...], second[...], scratch[...] * scale)
        scratch[...] = updated
        for slot, start in enumerate(starts):
            weights[:, start : start + LANES] = scratch[pl.ds(slot, part, stride=per), :].astype(weights.dtype)

    param_spec = pl.BlockSpec((part * per, LANES), lambda i, place: (place[0], 0))
    return call(
        kernel,
        [jax.ShapeDtypeStruct((part, width), jnp.bfloat16)] * 2,
        20 * part * width,
        20 * part * width,
        grid_spec=pltpu.PrefetchScalarGridSpec(
            num_scalar_prefetch=1,
            grid=(1,),
            in_specs=[full((8, LANES)), *[spec for _, spec in shares], param_spec, param_spec, param_spec],
            out_specs=[pl.BlockSpec((part, width), lambda i, place: (0, 0))] * 2,
            scratch_shapes=[pltpu.VMEM((part * per, LANES), jnp.float32)],
        ),
    )(place, count, *[a for a, _ in shares], *params)


def update_kernel(place, count, grad, master, first, second, new_master, new_first, new_second, scratch):
    rows, width = grad.shape
    per = width // LANES
    scale = 1.0 / count[0:1, 0:1]
    for slot, start in enumerate(slots(width // 2)):
        scratch[pl.ds(slot, rows, stride=per), :] = grad[:, start : start + LANES].astype(jnp.float32)
    updated, one, two = adamw(master[...], first[...], second[...], scratch[...] * scale)
    new_master[...] = updated
    new_first[...] = one
    new_second[...] = two


def update(me, count, grads, params, block):
    replicas, rows, width = grads.shape
    per = width // LANES
    steps = rows // block
    param_spec = pl.BlockSpec((block * per, LANES), lambda k, i, me: ((me[0] ^ k) * steps + i, 0))
    return call(
        update_kernel,
        [jax.ShapeDtypeStruct(params[0].shape, jnp.float32)] * 3,
        20 * replicas * rows * width,
        26 * replicas * rows * width,
        grid_spec=pltpu.PrefetchScalarGridSpec(
            num_scalar_prefetch=1,
            grid=(replicas, steps),
            in_specs=[
                full((8, LANES)),
                pl.BlockSpec((None, block, width), lambda k, i, me: (k, i, 0)),
                param_spec,
                param_spec,
                param_spec,
            ],
            out_specs=[param_spec] * 3,
            scratch_shapes=[pltpu.VMEM((block * per, LANES), jnp.float32)],
        ),
    )(me, count, grads, *params)


def combine(shares, pair, pairs):
    rows, width = shares[0][1].block_shape
    features, tokens = width // 2, rows // pairs
    per = width // LANES

    def kernel(pair, *refs):
        sources, out, scratch = refs[: len(shares)], refs[-2], refs[-1]
        for o in range(pairs):
            start = (pair[0] ^ o) * tokens
            for slot, column in enumerate(slots(features)):
                total = None
                for source in sources:
                    piece = source[o * tokens : (o + 1) * tokens, column : column + LANES].astype(jnp.float32)
                    total = piece if total is None else total + piece
                scratch[pl.ds(start * per + slot, tokens, stride=per), :] = total
        out[...] = scratch[...].astype(out.dtype)

    out = call(
        kernel,
        jax.ShapeDtypeStruct((rows * per, LANES), jnp.bfloat16),
        0,
        8 * rows * width,
        grid=(1,),
        in_specs=[SMEM] + [s for _, s in shares],
        out_specs=full((rows * per, LANES)),
        scratch_shapes=[pltpu.VMEM((rows * per, LANES), jnp.float32)],
    )(pair, *[a for a, _ in shares])
    return from_lane_rows(out, rows, features)


def after(value, *deps):
    return lax.optimization_barrier((value, *deps))[0] if deps else value


def swap(value, axis, k):
    if k == 0:
        return value
    return lax.ppermute(value, axis, [(i, i ^ k) for i in range(lax.axis_size(axis))])


def local(hidden_in, lengths, kv_grad_out, master, moment_one, moment_two):
    replicas, shards, pairs = (lax.axis_size(name) for name in ("rep", "shard", "tp"))
    rep, shard, pair = (lax.axis_index(name).astype(jnp.int32) for name in ("rep", "shard", "tp"))
    tokens, depth = hidden_in.shape
    block, _, features = kv_grad_out.shape
    width = 2 * features
    rows = depth // (shards * replicas)
    near = replicas // 2
    parities = [k for k in range(replicas) if k % 2] + [k for k in range(replicas) if not k % 2]
    odd = replicas // 2 * block

    order, k = [0], shards // 2
    while k:
        order, k = [i + k for i in order] + order, k // 2
    count_of_groups = max(1, min(GROUPS, rows // LANES))
    part = rows // count_of_groups
    groups = [(g * part, part, [shard ^ q for q in order]) for g in range(count_of_groups)]
    last_group = len(groups) - 1
    contract = (((0,), (0,)), ((), ()))

    def terms(here):
        return lax.dot_general(here, cotans, contract, preferred_element_type=jnp.float32).astype(jnp.bfloat16)

    def project(here, weights):
        return jnp.dot(here, weights, preferred_element_type=jnp.float32)

    pieces = pack(hidden_in, rep, groups[:1], replicas, rows)
    cotan, count = mask(kv_grad_out, jnp.stack([lengths[0], pair]), pairs)
    if last_group:
        pieces += pack(hidden_in, rep, groups[1:], replicas, rows)
    arrived, sides, line = [], [], []

    def travel(g, *waits):
        arrived.append(
            [pieces[g][0]]
            + [swap(after(h, *waits) if k >= near else h, "rep", k) for k, h in enumerate(pieces[g]) if k]
        )
        sides.append([])

    def pair_up(g, ks, *waits):
        for k in ks:
            sent = after(arrived[g][k], *line[-2:-1], *waits)
            sides[g].append([arrived[g][k]] + [swap(sent, "tp", o) for o in range(1, pairs)])
            line.append(sides[g][-1][-1])

    def lay(g):
        return jnp.concatenate([p for k in parities for p in sides[g][k]], axis=0)

    low, high = range(near), range(near, replicas)
    travel(0)
    pair_up(0, low)
    pair_up(0, high, cotan, *(pieces[1] if last_group else []))
    cotans = {0: cotan, near: swap(after(cotan, *arrived[0][near:], *line[:near]), "rep", near)}
    count, k = after(count, *arrived[0][near:]), 1
    while k < replicas:
        count, k = count + swap(count, "rep", k), 2 * k
    for g in range(1, len(groups)):
        travel(g, *([cotans[near]] if g == 1 else arrived[g - 1][near:]))
    if last_group:
        pair_up(1, low)
    k = near // 2
    while k:
        for have in list(cotans):
            cotans[have ^ k] = swap(cotans[have], "rep", k)
        k //= 2
    if last_group > 1:
        pair_up(2, low, cotans[near], count)
    cotans = jnp.concatenate([cotans[k] for k in parities], axis=0)
    k = 1
    while k < shards:
        count, k = count + swap(count, "shard", k), 2 * k

    params = [lane_rows(a) for a in (master, moment_one, moment_two)]
    spec = pl.BlockSpec((part, width), lambda i, place: (0, 0))
    inputs, sums, grads, fresh, products, total = [], [], [], [], [], None
    for g in range(len(groups)):
        here = after(lay(g), count)
        if g > 0:
            here = after(here, sums[g - 1][-1])
        if g > 1:
            here = after(here, fresh[g - 2])
        inputs.append(here)
        half = shards // 2 * part
        away = terms(here[:, :half])
        last = terms(after(here, away)[:, half:])
        if 0 < g + 1 <= last_group:
            pair_up(g + 1, high, last)
        if g + 3 <= last_group:
            pair_up(g + 3, low, last)
        shares, k = [last, swap(away, "shard", 1)], 2
        while k < shards:
            half //= 2
            sent = sum(v[:half].astype(jnp.float32) for v in shares).astype(jnp.bfloat16)
            shares, k = [v[half:] for v in shares] + [swap(sent, "shard", k)], 2 * k
        sums.append((shares, sent))
        place = (rep * len(groups) + g)[None]
        weights, grad = fresh_weights(place, count, [(v, spec) for v in shares], params)
        fresh.append(weights)
        grads.append(grad)
        k = shards // 2
        while k > 1:
            weights, k = jnp.concatenate([swap(weights, "shard", k), weights], axis=0), k // 2
        half = weights.shape[0]
        products.append((inputs[g][:, half:], weights))
        products.append((inputs[g][:, :half], swap(weights, "shard", 1)))

    every = {0: jnp.concatenate(grads, axis=0)}
    k = near
    while k:
        for have in list(every):
            every[have ^ k] = swap(every[have], "rep", k)
        k //= 2

    for here, weights in products[:-1]:
        product = project(here, weights)
        total = product if total is None else total + product
    here, weights = products[-1]
    here = after(here, every[near])
    away = project(here[:odd], weights)
    away = (away if total is None else total[:odd] + away).astype(jnp.bfloat16)
    stay = project(after(here, away)[odd:], weights)
    stay = (stay if total is None else total[odd:] + stay).astype(jnp.bfloat16)
    shares = [stay, swap(away, "rep", 1)]
    half, k = odd // 2, 2
    while k < replicas:
        sent = sum(v[half : 2 * half].astype(jnp.float32) for v in shares).astype(jnp.bfloat16)
        shares.append(swap(sent, "rep", k))
        half, k = half // 2, 2 * k
    fresh = combine([(v, full((block, width))) for v in shares], pair[None], pairs)

    every = jnp.stack([every[k] for k in range(replicas)])
    updated = update(rep[None], count, every, params, min(rows, 256))
    updated = [from_lane_rows(a, master.shape[0], features) for a in updated]
    return (*updated, fresh)


def solution(mesh):
    in_specs = (
        P(("rep", "shard", "tp"), None),
        P(("rep", "shard")),
        P(("rep", "shard"), None, "tp"),
        P("shard", None, "tp"),
        P("shard", None, "tp"),
        P("shard", None, "tp"),
    )
    out_specs = (
        P("shard", None, "tp"),
        P("shard", None, "tp"),
        P("shard", None, "tp"),
        P(("rep", "shard"), None, "tp"),
    )
    return jax.shard_map(local, mesh=mesh, in_specs=in_specs, out_specs=out_specs, check_vma=False)
```

time: 889 us -> 318 us (0.36)
  waiting for transfers between devices: 679 us -> 96.5 us
  local copies, waits for them, and re-layouts: 94.4 us -> 33.7 us
  Pallas kernels: 0 us -> 53.1 us
  starting transfers between devices: 0.16 us -> 50.3 us
  matrix products: 30.7 us -> 74.7 us
  blocking collectives: 35.1 us -> 0 us
  other arithmetic: 35 us -> 6.29 us
  between operations: 14.5 us -> 2.09 us
    all_gather x2 -> x0, waiting for transfers between devices: 344 us -> none  [the longest x1 239 us: local(): piece = lax.all_gather(weights, 'shard', axis=0, tiled=True)]
    reduce_scatter x1 -> x0, waiting for transfers between devices: 280 us -> none  [local(): lax.psum_scatter(lax.dot_general(columns, cotan, contract, preferred_elem...]
    ppermute x0 -> x56, waiting for transfers between devices: none -> 96.5 us  [swap(): lax.ppermute(value, axis, [(i, i ^ k) for i in range(lax.axis_size(axis))])]
    psum x1 -> x0, waiting for transfers between devices: 53.8 us -> none  [local(): summed = lax.psum(shard_grad, 'rep').astype(jnp.float32)]
    pallas_call x0 -> x9, Pallas kernels: none -> 53.1 us  [the longest x1 23.7 us: update(): call(update_kernel, [jax.ShapeDtypeStruct(params[0].shape, jnp.float32)]...]
    ppermute x0 -> x56, starting transfers between devices: none -> 50.3 us  [swap(): lax.ppermute(value, axis, [(i, i ^ k) for i in range(lax.axis_size(axis))])]
    unnamed x10 -> x126, local copies, waits for them, and re-layouts: 66.8 us -> 21.4 us
    dot_general x2 -> x17, matrix products: 30.7 us -> 74.7 us  [the longest x9 56.3 us: project(): return jnp.dot(here, weights, preferred_element_type=jnp.float32)]
  transfers between devices with their start and end apart: 4 -> 56, of which waited for: 4 -> 22; matrix products, arithmetic and copies ran while one was open for 6% -> 34% of each run, Pallas kernels for 0% -> 15%
where the time goes in v1:
time: 318 us; the launch traced here: 317 us
  waiting for transfers between devices  96.5 us (30%)
  matrix products  74.7 us (23%)
  Pallas kernels  53.1 us (17%)
  starting transfers between devices  50.3 us (16%)
  local copies, waits for them, and re-layouts  33.7 us (11%)
  other arithmetic  6.29 us (2%)
    ppermute x56, waiting for transfers between devices, swap(): lax.ppermute(value, axis, [(i, i ^ k) for i in range(lax.axis_size(axis))])  96.5 us
    dot_general x9, matrix products, project(): return jnp.dot(here, weights, preferred_element_type=jnp.float32)  56.3 us
    ppermute x56, starting transfers between devices, swap(): lax.ppermute(value, axis, [(i, i ^ k) for i in range(lax.axis_size(axis))])  50.3 us
    pallas_call x1, Pallas kernels, update(): call(update_kernel, [jax.ShapeDtypeStruct(params[0].shape, jnp.float32)]...  23.7 us
    unnamed x126, local copies, waits for them, and re-layouts  21.4 us
    dot_general x8, matrix products, terms(): lax.dot_general(here, cotans, contract, preferred_element_type=jnp.float32)  18.3 us
    pallas_call x4, Pallas kernels, fresh_weights(): call(kernel, [jax.ShapeDtypeStruct((part, width), jnp.bfloat16)] * 2, 20...  14.1 us
    pallas_call x2, Pallas kernels, pack(): call(kernel, [jax.ShapeDtypeStruct(shape, hidden.dtype) for shape in shap...  8.13 us
  transfers between devices with their start and end apart: 56, of which 22 were waited for; matrix products, arithmetic and copies ran while one was open for 34% of the time, Pallas kernels for 15%

profile of v1, /device:TPU:0, one launch (start us, length us, event | category | flops | bytes accessed | tf_op | source)
XLA Modules:
  0.0 316.7 jit_solution(3859849105039611486)
XLA Ops:
  1.3 3.1 shard_map.94
  10.8 3.2 %shard_map.93 = (bf16[512,1024]{1,0:T(8,128)(2,1)}, f32[8,128]{1,0:T(8,128)}) custom-call(s32[2]{0:T(128)} %pad_add_fusion.place, bf16[4096,128]{1,0:T(8,128)(2,1)} %bitcast.87), custom_call_target="tpu_custom_call" | custom-call | bytes 2097152 | tf_op jit(solution)/shard_map/pallas_call | solution.py:120
  16.8 3.3 %collective-permute-done = bf16[256,512]{1,0:T(8,128)(2,1)S(1)} collective-permute-done((bf16[256,512]{1,0:T(8,128)(2,1)}, bf16[256,512]{1,0:T(8,128)(2,1)S(1)}, u32[]{:S(2)}, u32[]{:S(2)}) %collective-permute-start) | collective-permute-done | bytes 262176 | tf_op jit(solution)/shard_map/ppermute | solution.py:240
  22.5 5.1 %shard_map.95 = (bf16[256,512]{1,0:T(8,128)(2,1)}, bf16[256,512]{1,0:T(8,128)(2,1)}, bf16[256,512]{1,0:T(8,128)(2,1)}, bf16[256,512]{1,0:T(8,128)(2,1)}, bf16[25...) custom-call(s32[13]{0:T(128)} %stack.60.place, ...), custom_call_target="tpu_custom_call" | custom-call | bytes 6291456 | tf_op jit(solution)/shard_map/pallas_call | solution.py:88
  33.2 13.0 %collective-permute-done.3 = f32[8,128]{1,0:T(8,128)S(1)} collective-permute-done((f32[8,128]{1,0:T(8,128)S(1)}, f32[8,128]{1,0:T(8,128)S(1)}, u32[]{:S(2)}, u32[]{:S(2)}) %collective-permute-start.3) | collective-permute-done | bytes 4128 | tf_op jit(solution)/shard_map/ppermute | solution.py:240
  58.4 4.7 %collective-permute-done.8 = bf16[256,512]{1,0:T(8,128)(2,1)S(1)} collective-permute-done((bf16[256,512]{1,0:T(8,128)(2,1)}, bf16[256,512]{1,0:T(8,128)(2,1)S(1)}, u32[]{:S(2)}, u32[]{:S(2)}) %collective-permute-start.8) | collective-permute-done | bytes 262176 | tf_op jit(solution)/shard_map/ppermute | solution.py:240
  65.3 3.4 %collective-permute-done.22 = bf16[256,512]{1,0:T(8,128)(2,1)S(1)} collective-permute-done((bf16[256,512]{1,0:T(8,128)(2,1)S(1)}, bf16[256,512]{1,0:T(8,128)(2,1)S(1)}, u32[]{:S(2)}, u32[]{:S(2)}) %collective-permute-start.22) | collective-permute-done | bytes 262176 | tf_op jit(solution)/shard_map/ppermute | solution.py:240
  68.7 5.6 %collective-permute-done.17 = bf16[256,512]{1,0:T(8,128)(2,1)S(1)} collective-permute-done((bf16[256,512]{1,0:T(8,128)(2,1)S(1)}, bf16[256,512]{1,0:T(8,128)(2,1)S(1)}, u32[]{:S(2)}, u32[]{:S(2)}) %collective-permute-start.17) | collective-permute-done | bytes 262176 | tf_op jit(solution)/shard_map/ppermute | solution.py:240
  84.6 4.6 %collective-permute-done.28 = bf16[256,512]{1,0:T(8,128)(2,1)S(1)} collective-permute-done((bf16[256,512]{1,0:T(8,128)(2,1)S(1)}, bf16[256,512]{1,0:T(8,128)(2,1)S(1)}, u32[]{:S(2)}, u32[]{:S(2)}) %collective-permute-start.28) | collective-permute-done | bytes 262176 | tf_op jit(solution)/shard_map/ppermute | solution.py:240
  96.8 8.4 %collective-permute-done.14 = bf16[256,1024]{1,0:T(8,128)(2,1)S(1)} collective-permute-done((bf16[256,1024]{1,0:T(8,128)(2,1)S(1)}, bf16[256,1024]{1,0:T(8,128)(2,1)S(1)}, u32[]{:S(2)}, u32[]{:S(2)}) %collective-permute-start.14) | collective-permute-done | bytes 524320 | tf_op jit(solution)/shard_map/ppermute | solution.py:240
  116.5 6.5 %collective-permute-done.34 = bf16[256,512]{1,0:T(8,128)(2,1)S(1)} collective-permute-done((bf16[256,512]{1,0:T(8,128)(2,1)S(1)}, bf16[256,512]{1,0:T(8,128)(2,1)S(1)}, u32[]{:S(2)}, u32[]{:S(2)}) %collective-permute-start.34) | collective-permute-done | bytes 262176 | tf_op jit(solution)/shard_map/ppermute | solution.py:240
  123.0 8.3 %collective-permute-done.15.refs_2_ = bf16[128,1024]{1,0:T(8,128)(2,1)S(1)} collective-permute-done((bf16[128,1024]{1,0:T(8,128)(2,1)S(1)}, bf16[128,1024]{1,0:T(8,128)(2,1)S(1)}, u32[]{:S(2)}, u32[]{:S(2)}) %collective-permute-start.15) | collective-permute-done | bytes 262176 | tf_op jit(solution)/shard_map/ppermute | solution.py:240
  132.0 3.5 %shard_map.96 = (bf16[128,1024]{1,0:T(8,128)(2,1)}, bf16[128,1024]{1,0:T(8,128)(2,1)}) custom-call(s32[1]{0:T(128)} %bitcast.9.place, f32[8,128]{1,0:T(8,128)} %add.63.count, bf16[128,1024]{1,0:T(8,128)(2,1)} %slice.140.refs_0_, bf16[128,1024]{1,0:T(8,128)(2,1)} %slice.141.refs_1_, bf16[128,1024]{1,0:T(8,128)(2,1)} %copy-done.11, f32[16384,128]{1,0:T(8,128)} %bitcast.71, ...), custom_call_target="tpu_custom_call" | custom-call | flops 2621440 | bytes 2621440 | tf_op jit(solution)/shard_map/pallas_call | solution.py:150
  135.5 3.4 %collective-permute-start.46 = (bf16[128,1024]{1,0:T(8,128)(2,1)}, bf16[128,1024]{1,0:T(8,128)(2,1)S(1)}, u32[]{:S(2)}, u32[]{:S(2)}) collective-permute-start(bf16[128,1024]{1,0:T(8,128)(2,1)} %get-tuple-element.113), channel_id=1, source_target_pairs={{0,4},{2,6},{4,0},{6,2},{1,5},{3,7},{5,1},{7,3},{8,12},{10,14},{12... | collective-permute-start | bytes 786440 | tf_op jit(solution)/shard_map/ppermute | solution.py:240
  140.6 4.6 %convolution_convert_fusion.3 = bf16[256,1024]{1,0:T(8,128)(2,1)} fusion(bf16[2048,1024]{1,0:T(8,128)(2,1)} %copy-done.14, bf16[2048,512]{1,0:T(8,128)(2,1)S(1)} %constant_dynamic-update-slice_fusion.20), kind=kOutput, calls=%fused_computation.10 | convolution fusion | flops 1074003968 | bytes 5767168 | tf_op jit(solution)/shard_map/dot_general | solution.py:264
  152.2 4.6 %fusion.10 = f32[2048,1024]{1,0:T(8,128)} fusion(bf16[256,1024]{1,0:T(8,128)(2,1)S(1)} %constant_dynamic-update-slice_fusion.40, bf16[2048,512]{1,0:T(8,128)(2,1)S(1)} %constant_dynamic-update-slice_fusion), kind=kOutput, calls=%fused_computation.21 | convolution fusion | flops 1073741824 | bytes 9961472 | tf_op jit(solution)/shard_map/dot_general | solution.py:267
  165.1 3.5 %shard_map.97 = (bf16[128,1024]{1,0:T(8,128)(2,1)}, bf16[128,1024]{1,0:T(8,128)(2,1)}) custom-call(s32[1]{0:T(128)} %bitcast.19.place, f32[8,128]{1,0:T(8,128)} %add.63.count, bf16[128,1024]{1,0:T(8,128)(2,1)} %slice.144.refs_0_, bf16[128,1024]{1,0:T(8,128)(2,1)} %slice.145.refs_1_, bf16[128,1024]{1,0:T(8,128)(2,1)} %copy-done.10, f32[16384,128]{1,0:T(8,128)} %bitcast.72, ...), custom_call_target="tpu_custom_call" | custom-call | flops 2621440 | bytes 2621440 | tf_op jit(solution)/shard_map/pallas_call | solution.py:150
  173.0 4.7 %convolution_convert_fusion.1 = bf16[256,1024]{1,0:T(8,128)(2,1)} fusion(bf16[2048,1024]{1,0:T(8,128)(2,1)} %copy-done.14, bf16[2048,512]{1,0:T(8,128)(2,1)} %constant_dynamic-update-slice_fusion.28), kind=kOutput, calls=%fused_computation.8 | convolution fusion | flops 1074003968 | bytes 5767168 | tf_op jit(solution)/shard_map/dot_general | solution.py:264
  185.2 3.5 %collective-permute-done.47 = bf16[256,1024]{1,0:T(8,128)(2,1)} collective-permute-done((bf16[256,1024]{1,0:T(8,128)(2,1)S(1)}, bf16[256,1024]{1,0:T(8,128)(2,1)}, u32[]{:S(2)}, u32[]{:S(2)}) %collective-permute-start.47) | collective-permute-done | bytes 524320 | tf_op jit(solution)/shard_map/ppermute | solution.py:240
  188.7 5.6 %fusion.22 = f32[2048,1024]{1,0:T(8,128)} fusion(bf16[256,1024]{1,0:T(8,128)(2,1)} %collective-permute-done.47, bf16[2048,512]{1,0:T(8,128)(2,1)S(1)} %constant_dynamic-update-slice_fusion), kind=kOutput, calls=%fused_computation.33 | convolution fusion | flops 1073741824 | bytes 9961472 | tf_op jit(solution)/shard_map/dot_general | solution.py:267
  194.4 4.6 %fusion.8 = f32[2048,1024]{1,0:T(8,128)} fusion(bf16[256,1024]{1,0:T(8,128)(2,1)S(1)} %constant_dynamic-update-slice_fusion.42, bf16[2048,512]{1,0:T(8,128)(2,1)S(1)} %constant_dynamic-update-slice_fusion.12), kind=kOutput, calls=%fused_computation.19 | convolution fusion | flops 1073741824 | bytes 9961472 | tf_op jit(solution)/shard_map/dot_general | solution.py:267
  199.7 3.6 %shard_map.98 = (bf16[128,1024]{1,0:T(8,128)(2,1)}, bf16[128,1024]{1,0:T(8,128)(2,1)}) custom-call(s32[1]{0:T(128)} %bitcast.26.place, f32[8,128]{1,0:T(8,128)} %add.63.count, bf16[128,1024]{1,0:T(8,128)(2,1)} %slice.148.refs_0_, bf16[128,1024]{1,0:T(8,128)(2,1)} %slice.149.refs_1_, bf16[128,1024]{1,0:T(8,128)(2,1)} %copy-done.12, f32[16384,128]{1,0:T(8,128)} %bitcast.73, ...), custom_call_target="tpu_custom_call" | custom-call | flops 2621440 | bytes 2621440 | tf_op jit(solution)/shard_map/pallas_call | solution.py:150
  210.6 14.2 %collective-permute-done.50 = bf16[128,1024]{1,0:T(8,128)(2,1)S(1)} collective-permute-done((bf16[128,1024]{1,0:T(8,128)(2,1)}, bf16[128,1024]{1,0:T(8,128)(2,1)S(1)}, u32[]{:S(2)}, u32[]{:S(2)}) %collective-permute-start.50) | collective-permute-done | bytes 262176 | tf_op jit(solution)/shard_map/ppermute | solution.py:240
  224.9 4.9 %fusion.6 = f32[2048,1024]{1,0:T(8,128)} fusion(bf16[256,1024]{1,0:T(8,128)(2,1)S(1)} %constant_dynamic-update-slice_fusion.44, bf16[2048,512]{1,0:T(8,128)(2,1)S(1)} %constant_dynamic-update-slice_fusion.20), kind=kOutput, calls=%fused_computation.17 | convolution fusion | flops 1073741824 | bytes 9961472 | tf_op jit(solution)/shard_map/dot_general | solution.py:267
  230.5 3.5 %shard_map.99 = (bf16[128,1024]{1,0:T(8,128)(2,1)}, bf16[128,1024]{1,0:T(8,128)(2,1)}) custom-call(s32[1]{0:T(128)} %bitcast.27.place, f32[8,128]{1,0:T(8,128)} %add.63.count, bf16[128,1024]{1,0:T(8,128)(2,1)} %slice.152.refs_0_, bf16[128,1024]{1,0:T(8,128)(2,1)} %slice.153.refs_1_, bf16[128,1024]{1,0:T(8,128)(2,1)} %copy-done.13, f32[16384,128]{1,0:T(8,128)} %bitcast.74, ...), custom_call_target="tpu_custom_call" | custom-call | flops 2621440 | bytes 2621440 | tf_op jit(solution)/shard_map/pallas_call | solution.py:150
  236.1 4.7 %fusion.19 = f32[2048,1024]{1,0:T(8,128)} fusion(bf16[256,1024]{1,0:T(8,128)(2,1)S(1)} %collective-permute-done.49, bf16[2048,512]{1,0:T(8,128)(2,1)S(1)} %constant_dynamic-update-slice_fusion.12), kind=kOutput, calls=%fused_computation.30 | convolution fusion | flops 1073741824 | bytes 9961472 | tf_op jit(solution)/shard_map/dot_general | solution.py:267
  242.0 5.7 %collective-permute-done.52 = bf16[128,1024]{1,0:T(8,128)(2,1)S(1)} collective-permute-done((bf16[128,1024]{1,0:T(8,128)(2,1)}, bf16[128,1024]{1,0:T(8,128)(2,1)S(1)}, u32[]{:S(2)}, u32[]{:S(2)}) %collective-permute-start.52) | collective-permute-done | bytes 262176 | tf_op jit(solution)/shard_map/ppermute | solution.py:240
  247.9 5.7 %fusion.16 = f32[2048,1024]{1,0:T(8,128)} fusion(bf16[256,1024]{1,0:T(8,128)(2,1)} %collective-permute-done.51, bf16[2048,512]{1,0:T(8,128)(2,1)S(1)} %constant_dynamic-update-slice_fusion.20), kind=kOutput, calls=%fused_computation.27 | convolution fusion | flops 1073741824 | bytes 9961472 | tf_op jit(solution)/shard_map/dot_general | solution.py:267
  253.6 20.6 %add_add_fusion = f32[2048,1024]{1,0:T(8,128)} fusion(f32[2048,1024]{1,0:T(8,128)} %fusion.16, f32[2048,1024]{1,0:T(8,128)} %fusion.6, f32[2048,1024]{1,0:T(8,128)} %fusion.19, f32[2048,1024]{1,0:T(8,128)} %fusion.8, f32[2048,1024]{1,0:T(8,128)} %fusion.10, f32[2048,1024]{1,0:T(8,128)} %fusion.22, ...), kind=kOutput, calls=%fused_computation | convolution fusion | flops 1086324736 | bytes 60293120 | tf_op jit(solution)/shard_map/dot_general | solution.py:267
  284.5 3.5 %pad_maximum_fusion.grad = bf16[4,512,1024]{2,1,0:T(8,128)(2,1)} fusion(bf16[1,512,1024]{2,1,0:T(8,128)(2,1)S(1)} %bitcast.89, bf16[1,512,1024]{2,1,0:T(8,128)(2,1)} %bitcast.30, bf16[1,512,1024]{2,1,0:T(8,128)(2,1)S(1)} %bitcast.88, bf16[1,512,1024]{2,1,0:T(8,128)(2,1)} %bitcast.28), kind=kLoop, calls=%fused_computation.5 | loop fusion | flops 6291456 | bytes 8388608 | tf_op jit(solution)/shard_map/stack | solution.py:373
  288.0 23.7 %shard_map.100 = (f32[16384,128]{1,0:T(8,128)}, f32[16384,128]{1,0:T(8,128)}, f32[16384,128]{1,0:T(8,128)}) custom-call(s32[1]{0:T(128)} %bitcast.place, f32[8,128]{1,0:T(8,128)} %add.63.count, bf16[4,512,1024]{2,1,0:T(8,128)(2,1)} %pad_maximum_fusion.grad, f32[16384,128]{1,0:T(8,128)} %bitcast.75, f32[16384,128]{1,0:T(8,128)} %bitcast.80, f32[16384,128]{1,0:T(8,128)} %bitcast.85), custom_call_target="tpu_custom_call" | custom-call | flops 41943040 | bytes 54525952 | tf_op jit(solution)/shard_map/pallas_call | solution.py:182
  312.7 4.0 %shard_map.101 = bf16[4096,128]{1,0:T(8,128)(2,1)} custom-call(s32[1]{0:T(128)} %bitcast.1.pair, bf16[1024,1024]{1,0:T(8,128)(2,1)} %copy-done, bf16[1024,1024]{1,0:T(8,128)(2,1)} %copy-done.1, bf16[512,1024]{1,0:T(8,128)(2,1)} %copy-done.2), custom_call_target="tpu_custom_call" | custom-call | bytes 4194304 | tf_op jit(solution)/shard_map/pallas_call | solution.py:220
  (264 shorter events, 113.4 us)
Async XLA Ops:
  9.4 12.1 %collective-permute-start.7 = (bf16[256,512]{1,0:T(8,128)(2,1)S(1)}, bf16[256,512]{1,0:T(8,128)(2,1)S(1)}, u32[]{:S(2)}, u32[]{:S(2)}) collective-permute-start(bf16[256,512]{1,0:T(8,128)(2,1)S(1)} %collective-permute-done.6), channel_id=1, source_target_pairs={{0,1},{1,0},{2,3},{3,2},{4,5},{5,4},{6,7},{7,6},{8,9},{9,8},{10,11... | collective-permute-start | bytes 786440 | tf_op jit(solution)/shard_map/ppermute | solution.py:240
  21.5 33.9 %collective-permute-start.12 = (bf16[512,1024]{1,0:T(8,128)(2,1)}, bf16[512,1024]{1,0:T(8,128)(2,1)}, u32[]{:S(2)}, u32[]{:S(2)}) collective-permute-start(bf16[512,1024]{1,0:T(8,128)(2,1)} %get-tuple-element.84), channel_id=1, source_target_pairs={{0,16},{8,24},{16,0},{24,8},{1,17},{9,25},{17,1},{25,9},{2,18},{10... | collective-permute-start | bytes 3145736 | tf_op jit(solution)/shard_map/ppermute | solution.py:240
  27.7 21.0 %collective-permute-start.19 = (bf16[256,512]{1,0:T(8,128)(2,1)}, bf16[256,512]{1,0:T(8,128)(2,1)}, u32[]{:S(2)}, u32[]{:S(2)}) collective-permute-start(bf16[256,512]{1,0:T(8,128)(2,1)} %get-tuple-element.89), channel_id=1, source_target_pairs={{0,8},{8,0},{16,24},{24,16},{1,9},{9,1},{17,25},{25,17},{2,10},{10... | collective-permute-start | bytes 786440 | tf_op jit(solution)/shard_map/ppermute | solution.py:240
  28.2 35.7 %collective-permute-start.11 = (bf16[512,1024]{1,0:T(8,128)(2,1)S(1)}, bf16[512,1024]{1,0:T(8,128)(2,1)}, u32[]{:S(2)}, u32[]{:S(2)}) collective-permute-start(bf16[512,1024]{1,0:T(8,128)(2,1)S(1)} %copy-done.3), channel_id=1, source_target_pairs={{0,8},{8,0},{16,24},{24,16},{1,9},{9,1},{17,25},{25,17},{2,10},{10... | collective-permute-start | bytes 3145736 | tf_op jit(solution)/shard_map/ppermute | solution.py:240
  29.6 25.4 %collective-permute-start.29 = (bf16[256,512]{1,0:T(8,128)(2,1)}, bf16[256,512]{1,0:T(8,128)(2,1)S(1)}, u32[]{:S(2)}, u32[]{:S(2)}) collective-permute-start(bf16[256,512]{1,0:T(8,128)(2,1)} %get-tuple-element.103), channel_id=1, source_target_pairs={{0,8},{8,0},{16,24},{24,16},{1,9},{9,1},{17,25},{25,17},{2,10},{10... | collective-permute-start | bytes 786440 | tf_op jit(solution)/shard_map/ppermute | solution.py:240
  30.4 15.8 %collective-permute-start.3 = (f32[8,128]{1,0:T(8,128)S(1)}, f32[8,128]{1,0:T(8,128)S(1)}, u32[]{:S(2)}, u32[]{:S(2)}) collective-permute-start(f32[8,128]{1,0:T(8,128)S(1)} %add.60), channel_id=1, source_target_pairs={{0,16},{8,24},{16,0},{24,8},{1,17},{9,25},{17,1},{25,9},{2,18},{10... | collective-permute-start | bytes 12296 | tf_op jit(solution)/shard_map/ppermute | solution.py:240
  55.5 21.3 %collective-permute-start.13 = (bf16[512,1024]{1,0:T(8,128)(2,1)}, bf16[512,1024]{1,0:T(8,128)(2,1)S(1)}, u32[]{:S(2)}, u32[]{:S(2)}) collective-permute-start(bf16[512,1024]{1,0:T(8,128)(2,1)} %collective-permute-done.12), channel_id=1, source_target_pairs={{0,8},{8,0},{16,24},{24,16},{1,9},{9,1},{17,25},{25,17},{2,10},{10... | collective-permute-start | bytes 3145736 | tf_op jit(solution)/shard_map/ppermute | solution.py:240
  68.7 12.1 %collective-permute-start.24 = (bf16[256,512]{1,0:T(8,128)(2,1)S(1)}, bf16[256,512]{1,0:T(8,128)(2,1)S(1)}, u32[]{:S(2)}, u32[]{:S(2)}) collective-permute-start(bf16[256,512]{1,0:T(8,128)(2,1)S(1)} %copy-done.19), channel_id=1, source_target_pairs={{0,1},{1,0},{2,3},{3,2},{4,5},{5,4},{6,7},{7,6},{8,9},{9,8},{10,11... | collective-permute-start | bytes 786440 | tf_op jit(solution)/shard_map/ppermute | solution.py:240
  75.0 14.2 %collective-permute-start.28 = (bf16[256,512]{1,0:T(8,128)(2,1)S(1)}, bf16[256,512]{1,0:T(8,128)(2,1)S(1)}, u32[]{:S(2)}, u32[]{:S(2)}) collective-permute-start(bf16[256,512]{1,0:T(8,128)(2,1)S(1)} %copy-done.40), channel_id=1, source_target_pairs={{0,24},{8,16},{16,8},{24,0},{1,25},{9,17},{17,9},{25,1},{2,26},{10... | collective-permute-start | bytes 786440 | tf_op jit(solution)/shard_map/ppermute | solution.py:240
  89.2 58.4 %collective-permute-start.39 = (bf16[256,512]{1,0:T(8,128)(2,1)}, bf16[256,512]{1,0:T(8,128)(2,1)}, u32[]{:S(2)}, u32[]{:S(2)}) collective-permute-start(bf16[256,512]{1,0:T(8,128)(2,1)} %get-tuple-element.121), channel_id=1, source_target_pairs={{0,16},{8,24},{16,0},{24,8},{1,17},{9,25},{17,1},{25,9},{2,18},{10... | collective-permute-start | bytes 786440 | tf_op jit(solution)/shard_map/ppermute | solution.py:240
  89.8 21.6 %collective-permute-start.37 = (bf16[256,512]{1,0:T(8,128)(2,1)S(1)}, bf16[256,512]{1,0:T(8,128)(2,1)}, u32[]{:S(2)}, u32[]{:S(2)}) collective-permute-start(bf16[256,512]{1,0:T(8,128)(2,1)S(1)} %copy-done.39), channel_id=1, source_target_pairs={{0,24},{8,16},{16,8},{24,0},{1,25},{9,17},{17,9},{25,1},{2,26},{10... | collective-permute-start | bytes 786440 | tf_op jit(solution)/shard_map/ppermute | solution.py:240
  90.7 14.5 %collective-permute-start.14 = (bf16[256,1024]{1,0:T(8,128)(2,1)S(1)}, bf16[256,1024]{1,0:T(8,128)(2,1)S(1)}, u32[]{:S(2)}, u32[]{:S(2)}) collective-permute-start(bf16[256,1024]{1,0:T(8,128)(2,1)S(1)} %convolution_convert_fusion.7), channel_id=1, source_target_pairs={{0,2},{2,0},{4,6},{6,4},{1,3},{3,1},{5,7},{7,5},{8,10},{10,8},{12,... | collective-permute-start | bytes 1572872 | tf_op jit(solution)/shard_map/ppermute | solution.py:240
  92.3 23.3 %collective-permute-start.33 = (bf16[256,512]{1,0:T(8,128)(2,1)S(1)}, bf16[256,512]{1,0:T(8,128)(2,1)S(1)}, u32[]{:S(2)}, u32[]{:S(2)}) collective-permute-start(bf16[256,512]{1,0:T(8,128)(2,1)S(1)} %copy-done.17), channel_id=1, source_target_pairs={{0,1},{1,0},{2,3},{3,2},{4,5},{5,4},{6,7},{7,6},{8,9},{9,8},{10,11... | collective-permute-start | bytes 786440 | tf_op jit(solution)/shard_map/ppermute | solution.py:240
  95.4 12.5 %collective-permute-start.30 = (bf16[256,512]{1,0:T(8,128)(2,1)S(1)}, bf16[256,512]{1,0:T(8,128)(2,1)S(1)}, u32[]{:S(2)}, u32[]{:S(2)}) collective-permute-start(bf16[256,512]{1,0:T(8,128)(2,1)S(1)} %collective-permute-done.29), channel_id=1, source_target_pairs={{0,1},{1,0},{2,3},{3,2},{4,5},{5,4},{6,7},{7,6},{8,9},{9,8},{10,11... | collective-permute-start | bytes 786440 | tf_op jit(solution)/shard_map/ppermute | solution.py:240
  113.1 27.4 %collective-permute-start.26 = (bf16[256,1024]{1,0:T(8,128)(2,1)S(1)}, bf16[256,1024]{1,0:T(8,128)(2,1)S(1)}, u32[]{:S(2)}, u32[]{:S(2)}) collective-permute-start(bf16[256,1024]{1,0:T(8,128)(2,1)S(1)} %convolution_convert_fusion.5), channel_id=1, source_target_pairs={{0,2},{2,0},{4,6},{6,4},{1,3},{3,1},{5,7},{7,5},{8,10},{10,8},{12,... | collective-permute-start | bytes 1572872 | tf_op jit(solution)/shard_map/ppermute | solution.py:240
  114.7 16.6 %collective-permute-start.15 = (bf16[128,1024]{1,0:T(8,128)(2,1)S(1)}, bf16[128,1024]{1,0:T(8,128)(2,1)S(1)}, u32[]{:S(2)}, u32[]{:S(2)}) collective-permute-start(bf16[128,1024]{1,0:T(8,128)(2,1)S(1)} %add_convert_fusion.4), channel_id=1, source_target_pairs={{0,4},{2,6},{4,0},{6,2},{1,5},{3,7},{5,1},{7,3},{8,12},{10,14},{12... | collective-permute-start | bytes 786440 | tf_op jit(solution)/shard_map/ppermute | solution.py:240
  135.5 14.2 %collective-permute-start.46 = (bf16[128,1024]{1,0:T(8,128)(2,1)}, bf16[128,1024]{1,0:T(8,128)(2,1)S(1)}, u32[]{:S(2)}, u32[]{:S(2)}) collective-permute-start(bf16[128,1024]{1,0:T(8,128)(2,1)} %get-tuple-element.113), channel_id=1, source_target_pairs={{0,4},{2,6},{4,0},{6,2},{1,5},{3,7},{5,1},{7,3},{8,12},{10,14},{12... | collective-permute-start | bytes 786440 | tf_op jit(solution)/shard_map/ppermute | solution.py:240
  145.2 27.7 %collective-permute-start.35 = (bf16[256,1024]{1,0:T(8,128)(2,1)}, bf16[256,1024]{1,0:T(8,128)(2,1)S(1)}, u32[]{:S(2)}, u32[]{:S(2)}) collective-permute-start(bf16[256,1024]{1,0:T(8,128)(2,1)} %convolution_convert_fusion.3), channel_id=1, source_target_pairs={{0,2},{2,0},{4,6},{6,4},{1,3},{3,1},{5,7},{7,5},{8,10},{10,8},{12,... | collective-permute-start | bytes 1572872 | tf_op jit(solution)/shard_map/ppermute | solution.py:240
  145.2 19.1 %collective-permute-start.27 = (bf16[128,1024]{1,0:T(8,128)(2,1)S(1)}, bf16[128,1024]{1,0:T(8,128)(2,1)S(1)}, u32[]{:S(2)}, u32[]{:S(2)}) collective-permute-start(bf16[128,1024]{1,0:T(8,128)(2,1)S(1)} %add_convert_fusion.3), channel_id=1, source_target_pairs={{0,4},{2,6},{4,0},{6,2},{1,5},{3,7},{5,1},{7,3},{8,12},{10,14},{12... | collective-permute-start | bytes 786440 | tf_op jit(solution)/shard_map/ppermute | solution.py:240
  147.7 15.9 %collective-permute-start.40 = (bf16[256,512]{1,0:T(8,128)(2,1)}, bf16[256,512]{1,0:T(8,128)(2,1)S(1)}, u32[]{:S(2)}, u32[]{:S(2)}) collective-permute-start(bf16[256,512]{1,0:T(8,128)(2,1)} %collective-permute-done.39), channel_id=1, source_target_pairs={{0,1},{1,0},{2,3},{3,2},{4,5},{5,4},{6,7},{7,6},{8,9},{9,8},{10,11... | collective-permute-start | bytes 786440 | tf_op jit(solution)/shard_map/ppermute | solution.py:240
  149.8 38.9 %collective-permute-start.47 = (bf16[256,1024]{1,0:T(8,128)(2,1)S(1)}, bf16[256,1024]{1,0:T(8,128)(2,1)}, u32[]{:S(2)}, u32[]{:S(2)}) collective-permute-start(bf16[256,1024]{1,0:T(8,128)(2,1)S(1)} %constant_dynamic-update-slice_fusion.40), channel_id=1, source_target_pairs={{0,2},{2,0},{4,6},{6,4},{1,3},{3,1},{5,7},{7,5},{8,10},{10,8},{12,... | collective-permute-start | bytes 1572872 | tf_op jit(solution)/shard_map/ppermute | solution.py:240
  168.6 25.7 %collective-permute-start.48 = (bf16[128,1024]{1,0:T(8,128)(2,1)}, bf16[128,1024]{1,0:T(8,128)(2,1)S(1)}, u32[]{:S(2)}, u32[]{:S(2)}) collective-permute-start(bf16[128,1024]{1,0:T(8,128)(2,1)} %get-tuple-element.125), channel_id=1, source_target_pairs={{0,4},{2,6},{4,0},{6,2},{1,5},{3,7},{5,1},{7,3},{8,12},{10,14},{12... | collective-permute-start | bytes 786440 | tf_op jit(solution)/shard_map/ppermute | solution.py:240
  177.8 27.2 %collective-permute-start.41 = (bf16[256,1024]{1,0:T(8,128)(2,1)}, bf16[256,1024]{1,0:T(8,128)(2,1)}, u32[]{:S(2)}, u32[]{:S(2)}) collective-permute-start(bf16[256,1024]{1,0:T(8,128)(2,1)} %convolution_convert_fusion.1), channel_id=1, source_target_pairs={{0,2},{2,0},{4,6},{6,4},{1,3},{3,1},{5,7},{7,5},{8,10},{10,8},{12,... | collective-permute-start | bytes 1572872 | tf_op jit(solution)/shard_map/ppermute | solution.py:240
  179.5 19.5 %collective-permute-start.36 = (bf16[128,1024]{1,0:T(8,128)(2,1)S(1)}, bf16[128,1024]{1,0:T(8,128)(2,1)S(1)}, u32[]{:S(2)}, u32[]{:S(2)}) collective-permute-start(bf16[128,1024]{1,0:T(8,128)(2,1)S(1)} %add_convert_fusion.2), channel_id=1, source_target_pairs={{0,4},{2,6},{4,0},{6,2},{1,5},{3,7},{5,1},{7,3},{8,12},{10,14},{12... | collective-permute-start | bytes 786440 | tf_op jit(solution)/shard_map/ppermute | solution.py:240
  194.4 41.8 %collective-permute-start.49 = (bf16[256,1024]{1,0:T(8,128)(2,1)S(1)}, bf16[256,1024]{1,0:T(8,128)(2,1)S(1)}, u32[]{:S(2)}, u32[]{:S(2)}) collective-permute-start(bf16[256,1024]{1,0:T(8,128)(2,1)S(1)} %constant_dynamic-update-slice_fusion.42), channel_id=1, source_target_pairs={{0,2},{2,0},{4,6},{6,4},{1,3},{3,1},{5,7},{7,5},{8,10},{10,8},{12,... | collective-permute-start | bytes 1572872 | tf_op jit(solution)/shard_map/ppermute | solution.py:240
  203.3 21.5 %collective-permute-start.50 = (bf16[128,1024]{1,0:T(8,128)(2,1)}, bf16[128,1024]{1,0:T(8,128)(2,1)S(1)}, u32[]{:S(2)}, u32[]{:S(2)}) collective-permute-start(bf16[128,1024]{1,0:T(8,128)(2,1)} %get-tuple-element.132), channel_id=1, source_target_pairs={{0,4},{2,6},{4,0},{6,2},{1,5},{3,7},{5,1},{7,3},{8,12},{10,14},{12... | collective-permute-start | bytes 786440 | tf_op jit(solution)/shard_map/ppermute | solution.py:240
  206.0 23.8 %collective-permute-start.42 = (bf16[128,1024]{1,0:T(8,128)(2,1)S(1)}, bf16[128,1024]{1,0:T(8,128)(2,1)S(1)}, u32[]{:S(2)}, u32[]{:S(2)}) collective-permute-start(bf16[128,1024]{1,0:T(8,128)(2,1)S(1)} %add_convert_fusion.1), channel_id=1, source_target_pairs={{0,4},{2,6},{4,0},{6,2},{1,5},{3,7},{5,1},{7,3},{8,12},{10,14},{12... | collective-permute-start | bytes 786440 | tf_op jit(solution)/shard_map/ppermute | solution.py:240
  224.9 23.0 %collective-permute-start.51 = (bf16[256,1024]{1,0:T(8,128)(2,1)S(1)}, bf16[256,1024]{1,0:T(8,128)(2,1)}, u32[]{:S(2)}, u32[]{:S(2)}) collective-permute-start(bf16[256,1024]{1,0:T(8,128)(2,1)S(1)} %constant_dynamic-update-slice_fusion.44), channel_id=1, source_target_pairs={{0,2},{2,0},{4,6},{6,4},{1,3},{3,1},{5,7},{7,5},{8,10},{10,8},{12,... | collective-permute-start | bytes 1572872 | tf_op jit(solution)/shard_map/ppermute | solution.py:240
  234.0 13.7 %collective-permute-start.52 = (bf16[128,1024]{1,0:T(8,128)(2,1)}, bf16[128,1024]{1,0:T(8,128)(2,1)S(1)}, u32[]{:S(2)}, u32[]{:S(2)}) collective-permute-start(bf16[128,1024]{1,0:T(8,128)(2,1)} %get-tuple-element.133), channel_id=1, source_target_pairs={{0,4},{2,6},{4,0},{6,2},{1,5},{3,7},{5,1},{7,3},{8,12},{10,14},{12... | collective-permute-start | bytes 786440 | tf_op jit(solution)/shard_map/ppermute | solution.py:240
  241.5 32.6 %collective-permute-start.44 = (bf16[512,1024]{1,0:T(8,128)(2,1)}, bf16[512,1024]{1,0:T(8,128)(2,1)}, u32[]{:S(2)}, u32[]{:S(2)}) collective-permute-start(bf16[512,1024]{1,0:T(8,128)(2,1)} %constant_dynamic-update-slice_fusion.36), channel_id=1, source_target_pairs={{0,16},{8,24},{16,0},{24,8},{1,17},{9,25},{17,1},{25,9},{2,18},{10... | collective-permute-start | bytes 3145736 | tf_op jit(solution)/shard_map/ppermute | solution.py:240
  247.8 26.3 %collective-permute-start.53 = (bf16[256,1024]{1,0:T(8,128)(2,1)S(1)}, bf16[256,1024]{1,0:T(8,128)(2,1)S(1)}, u32[]{:S(2)}, u32[]{:S(2)}) collective-permute-start(bf16[256,1024]{1,0:T(8,128)(2,1)S(1)} %constant_dynamic-update-slice_fusion.46), channel_id=1, source_target_pairs={{0,2},{2,0},{4,6},{6,4},{1,3},{3,1},{5,7},{7,5},{8,10},{10,8},{12,... | collective-permute-start | bytes 1572872 | tf_op jit(solution)/shard_map/ppermute | solution.py:240
  283.9 27.8 %collective-permute-start.55 = (bf16[512,1024]{1,0:T(8,128)(2,1)S(1)}, bf16[512,1024]{1,0:T(8,128)(2,1)S(1)}, u32[]{:S(2)}, u32[]{:S(2)}) collective-permute-start(bf16[512,1024]{1,0:T(8,128)(2,1)S(1)} %add_convert_fusion), channel_id=1, source_target_pairs={{0,16},{8,24},{16,0},{24,8},{1,17},{9,25},{17,1},{25,9},{2,18},{10... | collective-permute-start | bytes 3145736 | tf_op jit(solution)/shard_map/ppermute | solution.py:240
  (68 other events, 734.8 us)
